TPU v7x, 128 devices: a whole 4x4x4 slice. The times are simulated.
128 devices in a mesh: lon: 16 (over z, y_lo, core), lat: 8 (over x, y_hi).
Axes of the slice: x: 4, y: 4 (y_hi: 2, y_lo: 2; y = y_hi * 2 + y_lo), z: 4, core: 2. Of those that a mesh axis runs over, the one named last changes fastest.
Arguments:
- frames: bfloat16 [1, 1, 16, 2048, 1024], P(None, None, None, 'lon', 'lat'), may hold values from -6 to 6
- hidden_low: bfloat16 [1, 64, 2048, 1024], P(None, None, 'lon', 'lat'), may hold values from -0.8984375 to 0.8984375
- cell_low: float32 [1, 64, 2048, 1024], P(None, None, 'lon', 'lat'), may hold values from -4 to 4
- hidden_top: bfloat16 [1, 64, 2048, 1024], P(None, None, 'lon', 'lat'), may hold values from -0.8984375 to 0.8984375
- cell_top: float32 [1, 64, 2048, 1024], P(None, None, 'lon', 'lat'), may hold values from -4 to 4
- weight_low: bfloat16 [256, 720], replicated, may hold values from -0.21875 to 0.21875
- bias_low: float32 [256], replicated, may hold values from -3 to 3
- weight_top: bfloat16 [256, 1152], replicated, may hold values from -0.1875 to 0.1875
- bias_top: float32 [256], replicated, may hold values from -3 to 3
Outputs:
- top_states: bfloat16 [1, 1, 64, 2048, 1024], P(None, None, None, 'lon', 'lat')
- hidden_low_out: bfloat16 [1, 64, 2048, 1024], P(None, None, 'lon', 'lat')
- cell_low_out: float32 [1, 64, 2048, 1024], P(None, None, 'lon', 'lat')
- cell_top_out: float32 [1, 64, 2048, 1024], P(None, None, 'lon', 'lat')
All inputs are finite; a program needn't handle non-finite values.
Results may differ from a plain program's by a relative error of at most 0.0017.
Values may be sent and summed in bfloat16 or wider, within the bound.
A program may use at most 384 MiB of HBM per device.

v0:
```python
import functools

import jax
import jax.numpy as jnp
from jax import lax
from jax.experimental import pallas as pl
from jax.experimental.pallas import tpu as pltpu
from jax.sharding import PartitionSpec as P

CIN, HID, TILE, BX = 16, 64, 128, 16
CL = CIN + HID
CT = 2 * HID
NB = TILE // BX
PK = 2 * CL + HID
PA = CL + HID
F32, BF16 = jnp.float32, jnp.bfloat16
MESH = pl.DeviceIdType.MESH


def rot(block, shift):
    return pltpu.roll(block, shift % block.shape[1] if isinstance(shift, int) else shift, 1)


def lanes(shape):
    return lax.broadcasted_iota(jnp.int32, shape, 1)


def update(gates, cell):
    take = jnp.tanh(gates[0:HID])
    keep = jnp.tanh(gates[HID:2 * HID])
    cand = jnp.tanh(gates[2 * HID:3 * HID])
    show = jnp.tanh(gates[3 * HID:4 * HID])
    cell = 0.5 * ((keep + 1.0) * cell + (take + 1.0) * cand)
    return 0.5 * (show + 1.0) * jnp.tanh(cell), cell


def extended_weights(out, weight, bias, width):
    gate = lax.broadcasted_iota(jnp.int32, (4 * HID, 1), 0)
    half = jnp.where((gate >= 2 * HID) & (gate < 3 * HID), 1.0, 0.5)
    out[:, 0:width] = (weight * half).astype(BF16)
    spread = jnp.transpose(jnp.broadcast_to(bias, (TILE, 4 * HID))) * half
    high = spread.astype(BF16).astype(F32)
    mid = (spread - high).astype(BF16).astype(F32)
    low = spread - high - mid
    lane = lanes((4 * HID, TILE))
    tail = jnp.where(lane == 0, high, jnp.where(lane == 1, mid, jnp.where(lane == 2, low, 0.0)))
    out[:, width:width + 16] = tail[:, 0:16].astype(BF16)


def shifted(dest, at, base, width, stride, value, lane_lo, lane_hi):
    lane = lanes(value.shape)
    down = jnp.where(lane == 0, lane_lo, rot(value, 1))
    up = jnp.where(lane == TILE - 1, lane_hi, rot(value, TILE - 1))
    dest[at, base:base + width] = down.astype(BF16)
    dest[at, 2 * stride + base:2 * stride + base + width] = up.astype(BF16)


def interleaved(low, high):
    even = lax.rem(lanes(low.shape), 2) == 0
    high = rot(high, TILE - 1)
    return jnp.where(even, low, high), jnp.where(even, high, low)


def windows(source, first, second, width, weights):
    pair = jnp.concatenate(
        [source[pl.ds(first, 3)].reshape(width, TILE), source[pl.ds(second, 3)].reshape(width, TILE)], axis=1
    )
    ones = jnp.ones((16, 2 * TILE), BF16)
    return jnp.dot(weights[:, 0:width + 16], jnp.concatenate([pair, ones], axis=0), preferred_element_type=F32)


def lower_kernel(
    fr, hl, ht, cl, wl, bl,
    t_hid, t_ht, co, g_top, sp,
    frv, hlv, htv, clv, s_low, hid, strip, hs, g_low, wle, tmp,
    near_out, rest_out, cell_out, cor_out, lonb_out, lonf_out,
    near_in, rest_in, cell_in, cor_in, lonb_in, lonf_in,
    sem_in, sem_out, send_lat, recv_lat, send_cor, recv_cor, send_lon, recv_lon,
):
    nlon, nlat = lax.axis_size("lon"), lax.axis_size("lat")
    lon, lat = lax.axis_index("lon"), lax.axis_index("lat")
    loads = [
        pltpu.make_async_copy(src, dst, sem_in.at[k])
        for k, (src, dst) in enumerate(((fr, frv), (hl, hlv), (ht, htv)))
    ] + [
        pltpu.make_async_copy(cl.at[:, b * BX:(b + 1) * BX, :], clv.at[b], sem_in.at[3 + b]) for b in range(NB)
    ]
    for load in loads[0:2]:
        load.start()

    polars = [lat == 0, lat == nlat - 1]
    lat_targets, slots = [], []
    for side in range(2):
        to_lat = jnp.where(polars[side], lat, lat + (-1 if side == 0 else 1))
        shift = jnp.where(polars[side], nlon // 2, 0)
        slots.append(jnp.where(polars[side], side, 1 - side))
        lat_targets.append([(lax.rem(lon + shift + step + nlon, nlon), to_lat) for step in (-1, 0, 1)])
    lon_targets = [(lax.rem(lon + step + nlon, nlon), lat) for step in (-1, 1)]

    barrier = pltpu.get_barrier_semaphore()
    for target in lat_targets[0] + lat_targets[1] + lon_targets:
        pl.semaphore_signal(barrier, inc=1, device_id=target, device_id_type=MESH)

    row = lax.broadcasted_iota(jnp.int32, (16, TILE), 0)
    col = lax.broadcasted_iota(jnp.int32, (16, TILE), 1)
    wanted = jnp.where(row == 1, 1, jnp.where(row == 2, TILE - 1, jnp.where(row == 3, TILE - 2, 0)))
    pick = jnp.where((col == wanted) & (row < 4), 1.0, 0.0).astype(BF16)

    def columns(field, base, count):
        def step(k, carry):
            at = pl.multiple_of(k * 8, 8)
            found = lax.dot_general(
                pick, field[pl.ds(at, 8)].reshape(8 * TILE, TILE), (((1,), (1,)), ((), ())),
                preferred_element_type=F32,
            )
            for j in range(8):
                tmp[pl.ds(pl.multiple_of((base + at + j) * 8, 8), 8), :] = found[0:8, j * TILE:(j + 1) * TILE]
            return carry
        lax.fori_loop(0, count // 8, step, 0)

    def rows(field, count, base, whole):
        for side in range(2):
            start = 0 if side == 0 else TILE - BX
            tmp[0:count * BX, :] = field[:, start:start + BX, :].astype(F32).reshape(count * BX, TILE)
            first, second = (0, 1) if side == 0 else (BX - 1, BX - 2)
            lonb_out[side, base:base + count] = tmp[pl.ds(first, count, stride=BX), :].astype(BF16)
            if whole:
                lonb_out[side, CL + base:CL + base + count] = tmp[pl.ds(second, count, stride=BX), :].astype(BF16)

    copies = []

    def send(src, dst, send_sem, recv_sem, target):
        copies.append(pltpu.make_async_remote_copy(
            src_ref=src, dst_ref=dst, send_sem=send_sem, recv_sem=recv_sem,
            device_id=target, device_id_type=MESH))
        copies[-1].start()

    def received(src, dst, send_sem, recv_sem):
        pltpu.make_async_remote_copy(
            src_ref=src, dst_ref=dst, send_sem=send_sem, recv_sem=recv_sem,
            device_id=lon_targets[0], device_id_type=MESH).wait_recv()

    for load in loads[0:2]:
        load.wait()
    for load in loads[2:]:
        load.start()
    columns(frv, 0, CIN)
    columns(hlv, CIN, HID)
    for side in range(2):
        near_out[side] = tmp[pl.ds(2 * side, CL, stride=8), :].astype(BF16)
        rest_out[side, 0:CL] = tmp[pl.ds(2 * side + 1, CL, stride=8), :].astype(BF16)
    pl.semaphore_wait(barrier, 8)
    for side in range(2):
        send(near_out.at[side], near_in.at[slots[side]], send_lat.at[0, side], recv_lat.at[0, slots[side]],
             lat_targets[side][1])

    rows(frv, CIN, 0, True)
    rows(hlv, HID, CIN, True)
    loads[2].wait()
    rows(htv, HID, 2 * CL, False)
    for side in range(2):
        send(lonb_out.at[side], lonb_in.at[1 - side], send_lon.at[0, side], recv_lon.at[0, 1 - side],
             lon_targets[side])
    columns(htv, 0, HID)
    for side in range(2):
        rest_out[side, CL:PA] = tmp[pl.ds(2 * side, HID, stride=8), :].astype(BF16)
        send(rest_out.at[side], rest_in.at[slots[side]], send_lat.at[1, side], recv_lat.at[1, slots[side]],
             lat_targets[side][1])

    for load in loads[3:]:
        load.wait()

    def cell_columns(k, carry):
        for j in range(4):
            turned = jnp.transpose(jnp.concatenate([clv[b, k * 4 + j] for b in range(NB)], axis=0))
            at = pl.multiple_of((k * 4 + j) * 8, 8)
            tmp[pl.ds(at, 8), :] = jnp.where(
                lax.broadcasted_iota(jnp.int32, (8, TILE), 0) < 4, turned[0:8], turned[TILE - 8:TILE])
        return carry

    lax.fori_loop(0, HID // 4, cell_columns, 0)
    for side in range(2):
        cell_out[side] = tmp[pl.ds(7 * side, HID, stride=8), :]
    for side in range(2):
        block, first = (0, 0) if side == 0 else (NB - 1, BX - 1)
        lonf_out[side] = clv.at[block].reshape(HID * BX, TILE)[pl.ds(first, HID, stride=BX), :]

    for side in range(2):
        near = near_out[side].astype(F32)
        rest = rest_out[side].astype(F32)
        cell = cell_out[side]
        high = cell.astype(BF16).astype(F32)
        mid = (cell - high).astype(BF16).astype(F32)
        low = cell - high - mid
        pad = jnp.zeros((CL - HID, TILE), F32)
        wide = [near, near, rest[0:CL], rest[0:CL]] + [
            jnp.concatenate([part, pad], axis=0) for part in (rest[CL:PA], high, mid, low)]
        for step in range(2):
            ends = (0, 1) if step == 0 else (TILE - 1, TILE - 2)
            source = (ends[0], ends[1], ends[0], ends[1], ends[0], ends[0], ends[0], ends[0])
            lane = lanes((CL, TILE))
            package = jnp.zeros((CL, TILE), F32)
            for k in range(8):
                package = jnp.where(lane == k, rot(wide[k], k - source[k] + TILE), package)
            cor_out[side, step] = package.astype(BF16)
    for side in range(2):
        for step in range(2):
            send(cor_out.at[side, step], cor_in.at[slots[side], 1 - step], send_cor.at[side, step],
                 recv_cor.at[slots[side], 1 - step], lat_targets[side][2 * step])
    for side in range(2):
        send(cell_out.at[side], cell_in.at[slots[side]], send_lat.at[2, side], recv_lat.at[2, slots[side]],
             lat_targets[side][1])
        send(lonf_out.at[side], lonf_in.at[1 - side], send_lon.at[1, side], recv_lon.at[1, 1 - side],
             lon_targets[side])

    def relayout(b, carry):
        at = pl.multiple_of(b * BX, BX)
        s_low[pl.ds(at + 2, BX), CL:CL + CIN] = jnp.swapaxes(frv[:, pl.ds(at, BX), :], 0, 1)
        s_low[pl.ds(at + 2, BX), CL + CIN:2 * CL] = jnp.swapaxes(hlv[:, pl.ds(at, BX), :], 0, 1)
        hid[1, pl.ds(at, BX)] = jnp.swapaxes(htv[:, pl.ds(at, BX), :], 0, 1)
        return carry

    lax.fori_loop(0, NB, relayout, 0)
    saves = [pltpu.make_async_copy(hid.at[1], t_ht, sem_out.at[0, 0])]
    saves[0].start()
    extended_weights(wle, jnp.transpose(wl[...].astype(F32)), bl[...], 9 * CL)

    for slot in range(2):
        received(near_out.at[0], near_in.at[slot], send_lat.at[0, slot], recv_lat.at[0, slot])
    for k, tile in enumerate(interleaved(near_in[0].astype(F32), near_in[1].astype(F32))):
        g_low[k] = tile.astype(BF16)

    def shift_row(x, parity):
        halo = rot(g_low[parity].astype(F32), lax.rem(TILE - x, TILE))
        shifted(s_low, x + 2, 0, CL, CL, s_low[x + 2, CL:2 * CL].astype(F32), halo, halo)

    def shift_first(i, carry):
        for j in range(4):
            shift_row(BX + 4 * i + j, j % 2)
        return carry

    shift_row(BX - 1, 1)
    lax.fori_loop(0, BX // 4, shift_first, 0)

    def low_rows(b, i):
        x = b * BX + i
        ahead = lax.rem(b + 1, NB) * BX + i
        cells = clv.at[b].reshape(HID * BX, TILE)
        cell = jnp.concatenate([cells[pl.ds(i + j, HID, stride=BX), :] for j in range(2)], axis=1)
        hidden, cell = update(windows(s_low, x + 1, x + 2, 9 * CL, wle), cell)
        for j in range(2):
            shift_row(ahead + j, j)
            part = slice(j * TILE, (j + 1) * TILE)
            cells[pl.ds(i + j, HID, stride=BX), :] = cell[:, part]
            hid[0, x + j] = hidden[:, part].astype(BF16)

    def save_block(b):
        at = pl.multiple_of(b * BX, BX)
        return (
            pltpu.make_async_copy(clv.at[b], co.at[b], sem_out.at[1, b]),
            pltpu.make_async_copy(hid.at[0, pl.ds(at, BX)], t_hid.at[pl.ds(at, BX)], sem_out.at[2, b]),
        )

    def low_block(k, carry):
        b = lax.rem(k, NB)
        for i in range(0, BX, 2):
            low_rows(b, i)
        for save in save_block(b):
            save.start()
        return carry

    lax.fori_loop(1, NB - 1, low_block, 0)

    for slot in range(2):
        received(lonb_out.at[0], lonb_in.at[slot], send_lon.at[0, slot], recv_lon.at[0, slot])
        for step in range(2):
            received(cor_out.at[0, 0], cor_in.at[slot, step], send_cor.at[slot, step], recv_cor.at[slot, step])

    for at, side, far in ((1, 0, 0), (0, 0, 1), (130, 1, 0), (131, 1, 1)):
        value = lonb_in[side, far * CL:far * CL + CL].astype(F32)
        lo = rot(cor_in[0, side].astype(F32), TILE - far)
        hi = rot(cor_in[1, side].astype(F32), TILE - 1 - far)
        s_low[at, CL:2 * CL] = value.astype(BF16)
        shifted(s_low, at, 0, CL, CL, value, lo, hi)
    lax.fori_loop(NB - 1, NB + 1, low_block, 0)

    for slot in range(2):
        received(rest_out.at[0], rest_in.at[slot], send_lat.at[1, slot], recv_lat.at[1, slot])
        received(cell_out.at[0], cell_in.at[slot], send_lat.at[2, slot], recv_lat.at[2, slot])
        received(lonf_out.at[0], lonf_in.at[slot], send_lon.at[1, slot], recv_lon.at[1, slot])
    for side in range(2):
        lane = lanes((CL, TILE))
        west = cor_in[side, 0].astype(F32)
        east = cor_in[side, 1].astype(F32)
        near = jnp.concatenate([
            jnp.where(lane == TILE - 1, rot(west, TILE - 1), rot(west, TILE - 3)),
            near_in[side].astype(F32), east], axis=1)
        far = jnp.concatenate([
            jnp.where(lane == TILE - 1, rot(west, TILE - 3), rot(west, TILE - 5)),
            rest_in[side, 0:CL].astype(F32), rot(east, TILE - 2)], axis=1)
        edge = 0 if side == 0 else TILE - 1
        parts = [lonb_in[0, 0:CL], lonb_in[0, CL:2 * CL], lonb_in[1, 0:CL], lonb_in[1, CL:2 * CL]]
        parts = [part.astype(F32) for part in parts]
        mine = jnp.concatenate([
            jnp.where(lane == TILE - 1, rot(parts[0], TILE - 1 - edge), rot(parts[1], 2 * TILE - 2 - edge)),
            near_out[side].astype(F32),
            jnp.where(lane == 0, rot(parts[2], TILE - edge), rot(parts[3], TILE + 1 - edge))], axis=1)
        outer = jnp.where(polars[side], mine, far)
        inner = jnp.where(polars[side], far, mine)
        order = (outer, near, inner) if side == 0 else (inner, near, outer)
        for e in range(3):
            for a in range(3):
                at = (3 * a + e) * CL
                strip[at:at + CL, :] = rot(order[e], 1 - a).astype(BF16)
        gates = jnp.dot(
            wle[:, 0:9 * CL + 16],
            jnp.concatenate([strip[...], jnp.ones((16, 3 * TILE), BF16)], axis=0),
            preferred_element_type=F32,
        )
        west, east = west[0:HID], east[0:HID]
        cell = jnp.concatenate([
            rot(west, TILE - 6) + rot(west, TILE - 7) + rot(west, TILE - 8),
            cell_in[side],
            rot(east, TILE - 5) + rot(east, TILE - 6) + rot(east, TILE - 7)], axis=1)
        hs[side], _ = update(gates, cell)

    for k, tile in enumerate(interleaved(hs[0, :, TILE:2 * TILE], hs[1, :, TILE:2 * TILE])):
        g_top[k, 0:HID] = tile.astype(BF16)
    for k, tile in enumerate(interleaved(rest_in[0, CL:PA].astype(F32), rest_in[1, CL:PA].astype(F32))):
        g_top[k, HID:CT] = tile.astype(BF16)

    hidden, _ = update(windows(s_low, 0, 129, 9 * CL, wle), jnp.concatenate([lonf_in[0], lonf_in[1]], axis=1))
    for side in range(2):
        src = TILE - 1 if side == 0 else 0
        value = hidden[:, side * TILE:(side + 1) * TILE]
        lo = rot(hs[0, :, 2 * side * TILE:(2 * side + 1) * TILE], TILE - src)
        hi = rot(hs[1, :, 2 * side * TILE:(2 * side + 1) * TILE], 2 * TILE - 1 - src)
        sp[side, CT:CT + HID] = value.astype(BF16)
        shifted(sp, side, 0, HID, CT, value, lo, hi)
        value = lonb_in[side, 2 * CL:PK].astype(F32)
        lo = rot(cor_in[0, side, 0:HID].astype(F32), TILE - 4)
        hi = rot(cor_in[1, side, 0:HID].astype(F32), TILE - 5)
        sp[side, CT + HID:2 * CT] = value.astype(BF16)
        shifted(sp, side, HID, HID, CT, value, lo, hi)

    for copy in copies:
        copy.wait_send()
    for b in range(NB):
        for save in save_block(b):
            save.wait()
    saves[0].wait()


def lower_layer(fr, hl, ht, cl, wl, bl):
    anywhere = pl.BlockSpec(memory_space=pl.ANY)
    whole = pl.BlockSpec(memory_space=pltpu.VMEM)
    exchanged = [
        pltpu.VMEM((2, CL, TILE), BF16),
        pltpu.VMEM((2, PA, TILE), BF16),
        pltpu.VMEM((2, HID, TILE), F32),
        pltpu.VMEM((2, 2, CL, TILE), BF16),
        pltpu.VMEM((2, PK, TILE), BF16),
        pltpu.VMEM((2, HID, TILE), F32),
    ]
    return pl.pallas_call(
        lower_kernel,
        out_shape=(
            jax.ShapeDtypeStruct((TILE, HID, TILE), BF16),
            jax.ShapeDtypeStruct((TILE, HID, TILE), BF16),
            jax.ShapeDtypeStruct((NB, HID, BX, TILE), F32),
            jax.ShapeDtypeStruct((2, CT, TILE), BF16),
            jax.ShapeDtypeStruct((2, 3 * CT, TILE), BF16),
        ),
        in_specs=[anywhere] * 4 + [whole] * 2,
        out_specs=(anywhere, anywhere, anywhere, whole, whole),
        scratch_shapes=[
            pltpu.VMEM((CIN, TILE, TILE), BF16),
            pltpu.VMEM((HID, TILE, TILE), BF16),
            pltpu.VMEM((HID, TILE, TILE), BF16),
            pltpu.VMEM((NB, HID, BX, TILE), F32),
            pltpu.VMEM((TILE + 4, 3 * CL, TILE), BF16),
            pltpu.VMEM((2, TILE, HID, TILE), BF16),
            pltpu.VMEM((9 * CL, 3 * TILE), BF16),
            pltpu.VMEM((2, HID, 3 * TILE), F32),
            pltpu.VMEM((2, CL, TILE), BF16),
            pltpu.VMEM((4 * HID, 9 * CL + 48), BF16),
            pltpu.VMEM((HID * BX, TILE), F32),
            *exchanged,
            *exchanged,
            pltpu.SemaphoreType.DMA((3 + NB,)),
            pltpu.SemaphoreType.DMA((3, NB)),
            pltpu.SemaphoreType.DMA((3, 2)),
            pltpu.SemaphoreType.DMA((3, 2)),
            pltpu.SemaphoreType.DMA((2, 2)),
            pltpu.SemaphoreType.DMA((2, 2)),
            pltpu.SemaphoreType.DMA((2, 2)),
            pltpu.SemaphoreType.DMA((2, 2)),
        ],
        compiler_params=pltpu.CompilerParams(
            collective_id=0, has_side_effects=True, vmem_limit_bytes=60 * 1024 * 1024
        ),
        name="lower_layer",
    )(fr, hl, ht, cl, wl, bl)


def upper_kernel(
    t_hid, t_ht, co_in, ct, g_top, sp, wt, bt,
    th, ho, co, cto,
    ctv, cov, hov, thv, s_top, wte, rows,
    sem_in, sem_out,
):
    def span(b):
        return pl.ds(pl.multiple_of(b * BX, BX), BX)

    def load(k, b):
        if k >= 2:
            source, dest = (ct.at[:, span(b), :], ctv.at[b]) if k == 2 else (co_in.at[b], cov.at[b])
            return pltpu.make_async_copy(source, dest, sem_in.at[k, b])
        source = (t_hid, t_ht)[k]
        at = CT + k * HID
        return pltpu.make_async_copy(
            source.at[span(b)], s_top.at[pl.ds(b * BX + 1, BX), at:at + HID, :], sem_in.at[k, b])

    def save(k, b):
        source, dest = ((hov, ho), (thv, th), (ctv, cto), (cov, co))[k]
        return pltpu.make_async_copy(source.at[b], dest.at[:, span(b), :], sem_out.at[k, b])

    for b in range(2):
        for k in range(4):
            load(k, b).start()

    extended_weights(wte, wt[...].astype(F32), bt[...], 9 * CT)
    s_top[0] = sp[0]
    s_top[TILE + 1] = sp[1]

    def shift_row(x, parity):
        halo = rot(g_top[parity].astype(F32), lax.rem(TILE - x, TILE))
        shifted(s_top, x + 1, 0, CT, CT, s_top[x + 1, CT:2 * CT].astype(F32), halo, halo)

    for k in range(2):
        load(k, 0).wait()

    def shift_first(i, carry):
        for j in range(4):
            shift_row(4 * i + j, j % 2)
        return carry

    lax.fori_loop(0, BX // 4, shift_first, 0)

    def top_rows(b, i, shift):
        x = b * BX + i
        cells = ctv.at[b].reshape(HID * BX, TILE)
        cell = jnp.concatenate([cells[pl.ds(i + j, HID, stride=BX), :] for j in range(2)], axis=1)
        hidden, cell = update(windows(s_top, x, x + 1, 9 * CT, wte), cell)
        for j in range(2):
            if shift:
                shift_row(x + BX + j, j)
            part = slice(j * TILE, (j + 1) * TILE)
            cells[pl.ds(i + j, HID, stride=BX), :] = cell[:, part]
            rows[i + j] = hidden[:, part].astype(BF16)

    def top_block(b, shift):
        @pl.when(b + 2 < NB)
        def _():
            for k in range(4):
                load(k, b + 2).start()

        load(2, b).wait()
        if shift:
            for k in range(2):
                load(k, b + 1).wait()
        load(3, b).wait()
        hov[b] = jnp.swapaxes(s_top[pl.ds(b * BX + 1, BX), CT:CT + HID], 0, 1)
        before = jnp.maximum(b - 1, 0)
        thv[before] = jnp.swapaxes(rows[...], 0, 1)
        for i in range(0, BX, 2):
            top_rows(b, i, shift)
        for k in (0, 2, 3):
            save(k, b).start()

        @pl.when(b > 0)
        def _():
            save(1, before).start()

    def top_step(b, carry):
        top_block(b, True)
        return carry

    rows[...] = jnp.zeros(rows.shape, BF16)
    lax.fori_loop(0, NB - 1, top_step, 0)
    top_block(NB - 1, False)
    thv[NB - 1] = jnp.swapaxes(rows[...], 0, 1)
    save(1, NB - 1).start()
    for k in range(4):
        for b in range(NB):
            save(k, b).wait()


def upper_layer(t_hid, t_ht, co, ct, g_top, sp, wt, bt):
    anywhere = pl.BlockSpec(memory_space=pl.ANY)
    whole = pl.BlockSpec(memory_space=pltpu.VMEM)
    field = (HID, TILE, TILE)
    return pl.pallas_call(
        upper_kernel,
        out_shape=(
            jax.ShapeDtypeStruct(field, BF16),
            jax.ShapeDtypeStruct(field, BF16),
            jax.ShapeDtypeStruct(field, F32),
            jax.ShapeDtypeStruct(field, F32),
        ),
        in_specs=[anywhere] * 4 + [whole] * 4,
        out_specs=(anywhere,) * 4,
        scratch_shapes=[
            pltpu.VMEM((NB, HID, BX, TILE), F32),
            pltpu.VMEM((NB, HID, BX, TILE), F32),
            pltpu.VMEM((NB, HID, BX, TILE), BF16),
            pltpu.VMEM((NB, HID, BX, TILE), BF16),
            pltpu.VMEM((TILE + 2, 3 * CT, TILE), BF16),
            pltpu.VMEM((4 * HID, 9 * CT + TILE), BF16),
            pltpu.VMEM((BX, HID, TILE), BF16),
            pltpu.SemaphoreType.DMA((4, NB)),
            pltpu.SemaphoreType.DMA((4, NB)),
        ],
        compiler_params=pltpu.CompilerParams(vmem_limit_bytes=60 * 1024 * 1024),
        name="upper_layer",
    )(t_hid, t_ht, co, ct, g_top, sp, wt, bt)


def body(frames, hidden_low, cell_low, hidden_top, cell_top, weight_low, bias_low, weight_top, bias_top):
    fr = frames.reshape(frames.shape[2:])
    hl, cl, ht, ct = (field.reshape(field.shape[1:]) for field in (hidden_low, cell_low, hidden_top, cell_top))
    t_hid, t_ht, co, g_top, sp = lower_layer(fr, hl, ht, cl, weight_low.T, bias_low.reshape(1, -1))
    th, ho, co, cto = upper_layer(t_hid, t_ht, co, ct, g_top, sp, weight_top, bias_top.reshape(1, -1))
    return th[None, None], ho[None], co[None], cto[None]


def solution(mesh):
    field = P(None, None, "lon", "lat")
    frame = P(None, None, None, "lon", "lat")
    return jax.shard_map(
        body,
        mesh=mesh,
        in_specs=(frame, field, field, field, field, P(), P(), P(), P()),
        out_specs=(frame, field, field, field),
        check_vma=False,
    )
```

profile of v0, /device:TPU:2, one launch (start us, length us, event | category | flops | bytes accessed | tf_op | source)
XLA Modules:
  0.0 48.0 jit_solution(11658732967214734923)
XLA Ops:
  0.6 27.1 %lower_layer.1 = (bf16[128,64,128]{2,1,0:T(8,128)(2,1)}, bf16[128,64,128]{2,1,0:T(8,128)(2,1)}, f32[8,64,16,128]{3,2,1,0:T(8,128)}, bf16[2,128,128]{2,1,0:T(8,128)(2,1)}, bf16[2,384,128]{2,1,0:T(8,128)(2,1)}) custom-call(bf16[16,128,128]{2,1,0:T(8,128)(2,1)} %bitcast.16, bf16[64,128,128]{2,1,0:T(8,128)(2,1)} %bitcast.14, bf16[64,128,128]{2,1,0:T(8,128)(2,1)} %bitcast.15, ...), custom_call_target="tpu_custom_call" | custom-call | tf_op jit(solution)/shard_map/lower_layer/pallas_call | solution.py:365
  27.8 20.3 %upper_layer.1 = (bf16[64,128,128]{2,1,0:T(8,128)(2,1)}, bf16[64,128,128]{2,1,0:T(8,128)(2,1)}, f32[64,128,128]{2,1,0:T(8,128)}, f32[64,128,128]{2,1,0:T(8,128)}) custom-call(bf16[128,64,128]{2,1,0:T(8,128)(2,1)} %get-tuple-element.13.t_hid, bf16[128,64,128]{2,1,0:T(8,128)(2,1)} %get-tuple-element.14.t_ht, f32[8,64,16,128]{3,2,1,0:T(8,128)} %get-tuple-element.15.co_in, ...), custom_call_target="tpu_custom_call" | custom-call | tf_op jit(solution)/shard_map/upper_layer/pallas_call | solution.py:503
where the time goes:
time: 48.5 us; the launch traced here: 48 us
  Pallas kernels  47.4 us (98%)
  between operations  0.64 us (1%)
    pallas_call x1, Pallas kernels, lower_layer(): pl.pallas_call(lower_kernel, out_shape=(jax.ShapeDtypeStruct((TILE, HID,...  27.1 us
    pallas_call x1, Pallas kernels, upper_layer(): pl.pallas_call(upper_kernel, out_shape=(jax.ShapeDtypeStruct(field, BF16)...  20.3 us

commit v1 on v0

--- a/solution.py
+++ b/solution.py
@@ -11,6 +11,7 @@
 CL = CIN + HID
 CT = 2 * HID
 NB = TILE // BX
+PITCH = 24
 PK = 2 * CL + HID
 PA = CL + HID
 F32, BF16 = jnp.float32, jnp.bfloat16
@@ -72,7 +73,7 @@
 def lower_kernel(
     fr, hl, ht, cl, wl, bl,
     t_hid, t_ht, co, g_top, sp,
-    frv, hlv, htv, clv, s_low, hid, strip, hs, g_low, wle, tmp,
+    frv, hlv, htv, clv, s_low, hid, strip, hs, g_low, wle, tmp, ctmp,
     near_out, rest_out, cell_out, cor_out, lonb_out, lonf_out,
     near_in, rest_in, cell_in, cor_in, lonb_in, lonf_in,
     sem_in, sem_out, send_lat, recv_lat, send_cor, recv_cor, send_lon, recv_lon,
@@ -83,7 +84,7 @@
         pltpu.make_async_copy(src, dst, sem_in.at[k])
         for k, (src, dst) in enumerate(((fr, frv), (hl, hlv), (ht, htv)))
     ] + [
-        pltpu.make_async_copy(cl.at[:, b * BX:(b + 1) * BX, :], clv.at[b], sem_in.at[3 + b]) for b in range(NB)
+        pltpu.make_async_copy(cl.at[:, b * BX:(b + 1) * BX, :], clv.at[b, :, 0:BX, :], sem_in.at[3 + b]) for b in range(NB)
     ]
     for load in loads[0:2]:
         load.start()
@@ -106,17 +107,14 @@
     wanted = jnp.where(row == 1, 1, jnp.where(row == 2, TILE - 1, jnp.where(row == 3, TILE - 2, 0)))
     pick = jnp.where((col == wanted) & (row < 4), 1.0, 0.0).astype(BF16)
 
-    def columns(field, base, count):
-        def step(k, carry):
-            at = pl.multiple_of(k * 8, 8)
-            found = lax.dot_general(
-                pick, field[pl.ds(at, 8)].reshape(8 * TILE, TILE), (((1,), (1,)), ((), ())),
-                preferred_element_type=F32,
-            )
-            for j in range(8):
-                tmp[pl.ds(pl.multiple_of((base + at + j) * 8, 8), 8), :] = found[0:8, j * TILE:(j + 1) * TILE]
-            return carry
-        lax.fori_loop(0, count // 8, step, 0)
+    def columns(field, base, k):
+        at = pl.multiple_of(k * 8, 8)
+        found = lax.dot_general(
+            pick, field[pl.ds(at, 8)].reshape(8 * TILE, TILE), (((1,), (1,)), ((), ())),
+            preferred_element_type=F32,
+        )
+        for j in range(8):
+            tmp[pl.ds(pl.multiple_of((base + at + j) * 8, 8), 8), :] = found[0:8, j * TILE:(j + 1) * TILE]
 
     def rows(field, count, base, whole):
         for side in range(2):
@@ -144,8 +142,15 @@
         load.wait()
     for load in loads[2:]:
         load.start()
-    columns(frv, 0, CIN)
-    columns(hlv, CIN, HID)
+    for k in range(CIN // 8):
+        columns(frv, 0, k)
+
+    def hidden_columns(k, carry):
+        columns(hlv, CIN, 2 * k)
+        columns(hlv, CIN, 2 * k + 1)
+        return carry
+
+    lax.fori_loop(0, HID // 16, hidden_columns, 0)
     for side in range(2):
         near_out[side] = tmp[pl.ds(2 * side, CL, stride=8), :].astype(BF16)
         rest_out[side, 0:CL] = tmp[pl.ds(2 * side + 1, CL, stride=8), :].astype(BF16)
@@ -156,34 +161,36 @@
 
     rows(frv, CIN, 0, True)
     rows(hlv, HID, CIN, True)
+    extended_weights(wle, jnp.transpose(wl[...].astype(F32)), bl[...], 9 * CL)
     loads[2].wait()
     rows(htv, HID, 2 * CL, False)
     for side in range(2):
         send(lonb_out.at[side], lonb_in.at[1 - side], send_lon.at[0, side], recv_lon.at[0, 1 - side],
              lon_targets[side])
-    columns(htv, 0, HID)
+    for load in loads[3:]:
+        load.wait()
+
+    def relayout(b, carry):
+        at = pl.multiple_of(b * BX, BX)
+        columns(htv, 0, b)
+        for j in range(8):
+            turned = jnp.transpose(jnp.concatenate([clv[k, b * 8 + j, 0:BX] for k in range(NB)], axis=0))
+            ctmp[pl.ds(pl.multiple_of((b * 8 + j) * 8, 8), 8), :] = jnp.where(
+                lax.broadcasted_iota(jnp.int32, (8, TILE), 0) < 4, turned[0:8], turned[TILE - 8:TILE])
+        s_low[pl.ds(at + 2, BX), CL:CL + CIN] = jnp.swapaxes(frv[:, pl.ds(at, BX), :], 0, 1)
+        s_low[pl.ds(at + 2, BX), CL + CIN:2 * CL] = jnp.swapaxes(hlv[:, pl.ds(at, BX), :], 0, 1)
+        hid[1, pl.ds(at, BX)] = jnp.swapaxes(htv[:, pl.ds(at, BX), :], 0, 1)
+        return carry
+
+    lax.fori_loop(0, NB, relayout, 0)
     for side in range(2):
         rest_out[side, CL:PA] = tmp[pl.ds(2 * side, HID, stride=8), :].astype(BF16)
         send(rest_out.at[side], rest_in.at[slots[side]], send_lat.at[1, side], recv_lat.at[1, slots[side]],
              lat_targets[side][1])
-
-    for load in loads[3:]:
-        load.wait()
-
-    def cell_columns(k, carry):
-        for j in range(4):
-            turned = jnp.transpose(jnp.concatenate([clv[b, k * 4 + j] for b in range(NB)], axis=0))
-            at = pl.multiple_of((k * 4 + j) * 8, 8)
-            tmp[pl.ds(at, 8), :] = jnp.where(
-                lax.broadcasted_iota(jnp.int32, (8, TILE), 0) < 4, turned[0:8], turned[TILE - 8:TILE])
-        return carry
-
-    lax.fori_loop(0, HID // 4, cell_columns, 0)
-    for side in range(2):
-        cell_out[side] = tmp[pl.ds(7 * side, HID, stride=8), :]
+        cell_out[side] = ctmp[pl.ds(7 * side, HID, stride=8), :]
     for side in range(2):
         block, first = (0, 0) if side == 0 else (NB - 1, BX - 1)
-        lonf_out[side] = clv.at[block].reshape(HID * BX, TILE)[pl.ds(first, HID, stride=BX), :]
+        lonf_out[side] = clv.at[block].reshape(HID * PITCH, TILE)[pl.ds(first, HID, stride=PITCH), :]
 
     for side in range(2):
         near = near_out[side].astype(F32)
@@ -213,17 +220,8 @@
         send(lonf_out.at[side], lonf_in.at[1 - side], send_lon.at[1, side], recv_lon.at[1, 1 - side],
              lon_targets[side])
 
-    def relayout(b, carry):
-        at = pl.multiple_of(b * BX, BX)
-        s_low[pl.ds(at + 2, BX), CL:CL + CIN] = jnp.swapaxes(frv[:, pl.ds(at, BX), :], 0, 1)
-        s_low[pl.ds(at + 2, BX), CL + CIN:2 * CL] = jnp.swapaxes(hlv[:, pl.ds(at, BX), :], 0, 1)
-        hid[1, pl.ds(at, BX)] = jnp.swapaxes(htv[:, pl.ds(at, BX), :], 0, 1)
-        return carry
-
-    lax.fori_loop(0, NB, relayout, 0)
     saves = [pltpu.make_async_copy(hid.at[1], t_ht, sem_out.at[0, 0])]
     saves[0].start()
-    extended_weights(wle, jnp.transpose(wl[...].astype(F32)), bl[...], 9 * CL)
 
     for slot in range(2):
         received(near_out.at[0], near_in.at[slot], send_lat.at[0, slot], recv_lat.at[0, slot])
@@ -245,31 +243,34 @@
     def low_rows(b, i):
         x = b * BX + i
         ahead = lax.rem(b + 1, NB) * BX + i
-        cells = clv.at[b].reshape(HID * BX, TILE)
-        cell = jnp.concatenate([cells[pl.ds(i + j, HID, stride=BX), :] for j in range(2)], axis=1)
+        cells = clv.at[b].reshape(HID * PITCH, TILE)
+        cell = jnp.concatenate([cells[pl.ds(i + j, HID, stride=PITCH), :] for j in range(2)], axis=1)
         hidden, cell = update(windows(s_low, x + 1, x + 2, 9 * CL, wle), cell)
         for j in range(2):
             shift_row(ahead + j, j)
             part = slice(j * TILE, (j + 1) * TILE)
-            cells[pl.ds(i + j, HID, stride=BX), :] = cell[:, part]
+            cells[pl.ds(i + j, HID, stride=PITCH), :] = cell[:, part]
             hid[0, x + j] = hidden[:, part].astype(BF16)
 
     def save_block(b):
         at = pl.multiple_of(b * BX, BX)
         return (
-            pltpu.make_async_copy(clv.at[b], co.at[b], sem_out.at[1, b]),
+            pltpu.make_async_copy(clv.at[b, :, 0:BX, :], co.at[b], sem_out.at[1, b]),
             pltpu.make_async_copy(hid.at[0, pl.ds(at, BX)], t_hid.at[pl.ds(at, BX)], sem_out.at[2, b]),
         )
 
-    def low_block(k, carry):
-        b = lax.rem(k, NB)
+    def low_block(b):
         for i in range(0, BX, 2):
             low_rows(b, i)
         for save in save_block(b):
             save.start()
+
+    def low_step(k, carry):
+        low_block(2 * k + 1)
+        low_block(2 * k + 2)
         return carry
 
-    lax.fori_loop(1, NB - 1, low_block, 0)
+    lax.fori_loop(0, NB // 2 - 1, low_step, 0)
 
     for slot in range(2):
         received(lonb_out.at[0], lonb_in.at[slot], send_lon.at[0, slot], recv_lon.at[0, slot])
@@ -282,7 +283,8 @@
         hi = rot(cor_in[1, side].astype(F32), TILE - 1 - far)
         s_low[at, CL:2 * CL] = value.astype(BF16)
         shifted(s_low, at, 0, CL, CL, value, lo, hi)
-    lax.fori_loop(NB - 1, NB + 1, low_block, 0)
+    low_block(NB - 1)
+    low_block(0)
 
     for slot in range(2):
         received(rest_out.at[0], rest_in.at[slot], send_lat.at[1, slot], recv_lat.at[1, slot])
@@ -377,7 +379,7 @@
             pltpu.VMEM((CIN, TILE, TILE), BF16),
             pltpu.VMEM((HID, TILE, TILE), BF16),
             pltpu.VMEM((HID, TILE, TILE), BF16),
-            pltpu.VMEM((NB, HID, BX, TILE), F32),
+            pltpu.VMEM((NB, HID, PITCH, TILE), F32),
             pltpu.VMEM((TILE + 4, 3 * CL, TILE), BF16),
             pltpu.VMEM((2, TILE, HID, TILE), BF16),
             pltpu.VMEM((9 * CL, 3 * TILE), BF16),
@@ -385,6 +387,7 @@
             pltpu.VMEM((2, CL, TILE), BF16),
             pltpu.VMEM((4 * HID, 9 * CL + 48), BF16),
             pltpu.VMEM((HID * BX, TILE), F32),
+            pltpu.VMEM((HID * 8, TILE), F32),
             *exchanged,
             *exchanged,
             pltpu.SemaphoreType.DMA((3 + NB,)),
@@ -414,7 +417,7 @@
 
     def load(k, b):
         if k >= 2:
-            source, dest = (ct.at[:, span(b), :], ctv.at[b]) if k == 2 else (co_in.at[b], cov.at[b])
+            source, dest = (ct.at[:, span(b), :], ctv.at[b, :, 0:BX, :]) if k == 2 else (co_in.at[b], cov.at[b])
             return pltpu.make_async_copy(source, dest, sem_in.at[k, b])
         source = (t_hid, t_ht)[k]
         at = CT + k * HID
@@ -423,7 +426,8 @@
 
     def save(k, b):
         source, dest = ((hov, ho), (thv, th), (ctv, cto), (cov, co))[k]
-        return pltpu.make_async_copy(source.at[b], dest.at[:, span(b), :], sem_out.at[k, b])
+        source = source.at[b, :, 0:BX, :] if k == 2 else source.at[b]
+        return pltpu.make_async_copy(source, dest.at[:, span(b), :], sem_out.at[k, b])
 
     for b in range(2):
         for k in range(4):
@@ -439,6 +443,9 @@
 
     for k in range(2):
         load(k, 0).wait()
+    for b in range(2, 4):
+        for k in range(4):
+            load(k, b).start()
 
     def shift_first(i, carry):
         for j in range(4):
@@ -449,48 +456,65 @@
 
     def top_rows(b, i, shift):
         x = b * BX + i
-        cells = ctv.at[b].reshape(HID * BX, TILE)
-        cell = jnp.concatenate([cells[pl.ds(i + j, HID, stride=BX), :] for j in range(2)], axis=1)
+        cells = ctv.at[b].reshape(HID * PITCH, TILE)
+        cell = jnp.concatenate([cells[pl.ds(i + j, HID, stride=PITCH), :] for j in range(2)], axis=1)
         hidden, cell = update(windows(s_top, x, x + 1, 9 * CT, wte), cell)
         for j in range(2):
             if shift:
                 shift_row(x + BX + j, j)
             part = slice(j * TILE, (j + 1) * TILE)
-            cells[pl.ds(i + j, HID, stride=BX), :] = cell[:, part]
+            cells[pl.ds(i + j, HID, stride=PITCH), :] = cell[:, part]
             rows[i + j] = hidden[:, part].astype(BF16)
 
-    def top_block(b, shift):
-        @pl.when(b + 2 < NB)
-        def _():
-            for k in range(4):
-                load(k, b + 2).start()
-
-        load(2, b).wait()
-        if shift:
-            for k in range(2):
-                load(k, b + 1).wait()
-        load(3, b).wait()
+    def top_block(b, shift, before):
         hov[b] = jnp.swapaxes(s_top[pl.ds(b * BX + 1, BX), CT:CT + HID], 0, 1)
-        before = jnp.maximum(b - 1, 0)
         thv[before] = jnp.swapaxes(rows[...], 0, 1)
         for i in range(0, BX, 2):
             top_rows(b, i, shift)
         for k in (0, 2, 3):
             save(k, b).start()
 
-        @pl.when(b > 0)
+    def arrived(k, b):
+        for kind in k:
+            load(kind, b).wait()
+
+    def top_step(step, carry):
+        b = 2 * step
+
+        @pl.when(step > 0)
         def _():
-            save(1, before).start()
-
-    def top_step(b, carry):
-        top_block(b, True)
+            save(1, b - 2).start()
+
+        @pl.when(b + 4 < NB)
+        def _():
+            for k in range(4):
+                load(k, b + 4).start()
+                load(k, b + 5).start()
+
+        arrived((2, 3), b)
+        arrived((0, 1, 2, 3), b + 1)
+        arrived((0, 1), b + 2)
+        before = jnp.maximum(b - 1, 0)
+        top_block(b, True, before)
+        top_block(b + 1, True, b)
+
+        @pl.when(step > 0)
+        def _():
+            save(1, b - 1).start()
         return carry
 
     rows[...] = jnp.zeros(rows.shape, BF16)
-    lax.fori_loop(0, NB - 1, top_step, 0)
-    top_block(NB - 1, False)
-    thv[NB - 1] = jnp.swapaxes(rows[...], 0, 1)
-    save(1, NB - 1).start()
+    lax.fori_loop(0, NB // 2 - 1, top_step, 0)
+    b = NB - 2
+    save(1, b - 2).start()
+    arrived((2, 3), b)
+    arrived((0, 1, 2, 3), b + 1)
+    top_block(b, True, b - 1)
+    save(1, b - 1).start()
+    top_block(b + 1, False, b)
+    save(1, b).start()
+    thv[b + 1] = jnp.swapaxes(rows[...], 0, 1)
+    save(1, b + 1).start()
     for k in range(4):
         for b in range(NB):
             save(k, b).wait()
@@ -511,7 +535,7 @@
         in_specs=[anywhere] * 4 + [whole] * 4,
         out_specs=(anywhere,) * 4,
         scratch_shapes=[
-            pltpu.VMEM((NB, HID, BX, TILE), F32),
+            pltpu.VMEM((NB, HID, PITCH, TILE), F32),
             pltpu.VMEM((NB, HID, BX, TILE), F32),
             pltpu.VMEM((NB, HID, BX, TILE), BF16),
             pltpu.VMEM((NB, HID, BX, TILE), BF16),

time: 48.5 us -> 44.7 us (0.922)
  Pallas kernels: 47.4 us -> 43.7 us
    pallas_call x1, Pallas kernels: 27.1 us -> 24.8 us  [lower_layer(): pl.pallas_call(lower_kernel, out_shape=(jax.ShapeDtypeStruct((TILE, HID,...]
    pallas_call x1, Pallas kernels: 20.3 us -> 18.8 us  [upper_layer(): pl.pallas_call(upper_kernel, out_shape=(jax.ShapeDtypeStruct(field, BF16)...]
where the time goes in v1:
time: 44.7 us; the launch traced here: 44.5 us
  Pallas kernels  43.7 us (98%)
  between operations  0.8 us (2%)
    pallas_call x1, Pallas kernels, lower_layer(): pl.pallas_call(lower_kernel, out_shape=(jax.ShapeDtypeStruct((TILE, HID,...  24.8 us
    pallas_call x1, Pallas kernels, upper_layer(): pl.pallas_call(upper_kernel, out_shape=(jax.ShapeDtypeStruct(field, BF16)...  18.8 us

profile of v1, /device:TPU:2, one launch (start us, length us, event | category | flops | bytes accessed | tf_op | source)
XLA Modules:
  0.0 44.5 jit_solution(17474300465118818317)
XLA Ops:
  0.6 24.8 %lower_layer.1 = (bf16[128,64,128]{2,1,0:T(8,128)(2,1)}, bf16[128,64,128]{2,1,0:T(8,128)(2,1)}, f32[8,64,16,128]{3,2,1,0:T(8,128)}, bf16[2,128,128]{2,1,0:T(8,128)(2,1)}, bf16[2,384,128]{2,1,0:T(8,128)(2,1)}) custom-call(bf16[16,128,128]{2,1,0:T(8,128)(2,1)} %bitcast.16, bf16[64,128,128]{2,1,0:T(8,128)(2,1)} %bitcast.14, bf16[64,128,128]{2,1,0:T(8,128)(2,1)} %bitcast.15, ...), custom_call_target="tpu_custom_call" | custom-call | tf_op jit(solution)/shard_map/lower_layer/pallas_call | solution.py:367
  25.5 18.8 %upper_layer.1 = (bf16[64,128,128]{2,1,0:T(8,128)(2,1)}, bf16[64,128,128]{2,1,0:T(8,128)(2,1)}, f32[64,128,128]{2,1,0:T(8,128)}, f32[64,128,128]{2,1,0:T(8,128)}) custom-call(bf16[128,64,128]{2,1,0:T(8,128)(2,1)} %get-tuple-element.13.t_hid, bf16[128,64,128]{2,1,0:T(8,128)(2,1)} %get-tuple-element.14.t_ht, f32[8,64,16,128]{3,2,1,0:T(8,128)} %get-tuple-element.15.co_in, ...), custom_call_target="tpu_custom_call" | custom-call | tf_op jit(solution)/shard_map/upper_layer/pallas_call | solution.py:527

commit v2 on v1

--- a/solution.py
+++ b/solution.py
@@ -11,6 +11,7 @@
 CL = CIN + HID
 CT = 2 * HID
 NB = TILE // BX
+AHEAD = 4
 PITCH = 24
 PK = 2 * CL + HID
 PA = CL + HID
@@ -193,6 +194,58 @@
         lonf_out[side] = clv.at[block].reshape(HID * PITCH, TILE)[pl.ds(first, HID, stride=PITCH), :]
 
     for side in range(2):
+        send(cell_out.at[side], cell_in.at[slots[side]], send_lat.at[2, side], recv_lat.at[2, slots[side]],
+             lat_targets[side][1])
+        send(lonf_out.at[side], lonf_in.at[1 - side], send_lon.at[1, side], recv_lon.at[1, 1 - side],
+             lon_targets[side])
+
+    saves = [pltpu.make_async_copy(hid.at[1], t_ht, sem_out.at[0, 0])]
+    saves[0].start()
+
+    for slot in range(2):
+        received(near_out.at[0], near_in.at[slot], send_lat.at[0, slot], recv_lat.at[0, slot])
+    for k, tile in enumerate(interleaved(near_in[0].astype(F32), near_in[1].astype(F32))):
+        g_low[k] = tile.astype(BF16)
+
+    def shift_row(x, parity):
+        halo = rot(g_low[parity].astype(F32), lax.rem(TILE - x, TILE))
+        shifted(s_low, x + 2, 0, CL, CL, s_low[x + 2, CL:2 * CL].astype(F32), halo, halo)
+
+    for row in range(BX - 1, BX + AHEAD):
+        shift_row(row, row % 2)
+
+    def low_rows(b, i):
+        x = b * BX + i
+        ahead = (x + AHEAD) % TILE if isinstance(b, int) else x + AHEAD
+        cells = clv.at[b].reshape(HID * PITCH, TILE)
+        cell = jnp.concatenate([cells[pl.ds(i + j, HID, stride=PITCH), :] for j in range(2)], axis=1)
+        hidden, cell = update(windows(s_low, x + 1, x + 2, 9 * CL, wle), cell)
+        for j in range(2):
+            shift_row(ahead + j, j)
+            part = slice(j * TILE, (j + 1) * TILE)
+            cells[pl.ds(i + j, HID, stride=PITCH), :] = cell[:, part]
+            hid[0, x + j] = hidden[:, part].astype(BF16)
+
+    def save_block(b):
+        at = pl.multiple_of(b * BX, BX)
+        return (
+            pltpu.make_async_copy(clv.at[b, :, 0:BX, :], co.at[b], sem_out.at[1, b]),
+            pltpu.make_async_copy(hid.at[0, pl.ds(at, BX)], t_hid.at[pl.ds(at, BX)], sem_out.at[2, b]),
+        )
+
+    def low_block(b):
+        for i in range(0, BX, 2):
+            low_rows(b, i)
+        for save in save_block(b):
+            save.start()
+
+    def low_step(k, carry):
+        low_block(2 * k + 1)
+        low_block(2 * k + 2)
+        return carry
+
+    low_block(1)
+    for side in range(2):
         near = near_out[side].astype(F32)
         rest = rest_out[side].astype(F32)
         cell = cell_out[side]
@@ -214,63 +267,8 @@
         for step in range(2):
             send(cor_out.at[side, step], cor_in.at[slots[side], 1 - step], send_cor.at[side, step],
                  recv_cor.at[slots[side], 1 - step], lat_targets[side][2 * step])
-    for side in range(2):
-        send(cell_out.at[side], cell_in.at[slots[side]], send_lat.at[2, side], recv_lat.at[2, slots[side]],
-             lat_targets[side][1])
-        send(lonf_out.at[side], lonf_in.at[1 - side], send_lon.at[1, side], recv_lon.at[1, 1 - side],
-             lon_targets[side])
-
-    saves = [pltpu.make_async_copy(hid.at[1], t_ht, sem_out.at[0, 0])]
-    saves[0].start()
-
-    for slot in range(2):
-        received(near_out.at[0], near_in.at[slot], send_lat.at[0, slot], recv_lat.at[0, slot])
-    for k, tile in enumerate(interleaved(near_in[0].astype(F32), near_in[1].astype(F32))):
-        g_low[k] = tile.astype(BF16)
-
-    def shift_row(x, parity):
-        halo = rot(g_low[parity].astype(F32), lax.rem(TILE - x, TILE))
-        shifted(s_low, x + 2, 0, CL, CL, s_low[x + 2, CL:2 * CL].astype(F32), halo, halo)
-
-    def shift_first(i, carry):
-        for j in range(4):
-            shift_row(BX + 4 * i + j, j % 2)
-        return carry
-
-    shift_row(BX - 1, 1)
-    lax.fori_loop(0, BX // 4, shift_first, 0)
-
-    def low_rows(b, i):
-        x = b * BX + i
-        ahead = lax.rem(b + 1, NB) * BX + i
-        cells = clv.at[b].reshape(HID * PITCH, TILE)
-        cell = jnp.concatenate([cells[pl.ds(i + j, HID, stride=PITCH), :] for j in range(2)], axis=1)
-        hidden, cell = update(windows(s_low, x + 1, x + 2, 9 * CL, wle), cell)
-        for j in range(2):
-            shift_row(ahead + j, j)
-            part = slice(j * TILE, (j + 1) * TILE)
-            cells[pl.ds(i + j, HID, stride=PITCH), :] = cell[:, part]
-            hid[0, x + j] = hidden[:, part].astype(BF16)
-
-    def save_block(b):
-        at = pl.multiple_of(b * BX, BX)
-        return (
-            pltpu.make_async_copy(clv.at[b, :, 0:BX, :], co.at[b], sem_out.at[1, b]),
-            pltpu.make_async_copy(hid.at[0, pl.ds(at, BX)], t_hid.at[pl.ds(at, BX)], sem_out.at[2, b]),
-        )
-
-    def low_block(b):
-        for i in range(0, BX, 2):
-            low_rows(b, i)
-        for save in save_block(b):
-            save.start()
-
-    def low_step(k, carry):
-        low_block(2 * k + 1)
-        low_block(2 * k + 2)
-        return carry
-
-    lax.fori_loop(0, NB // 2 - 1, low_step, 0)
+    low_block(2)
+    lax.fori_loop(1, NB // 2 - 1, low_step, 0)
 
     for slot in range(2):
         received(lonb_out.at[0], lonb_in.at[slot], send_lon.at[0, slot], recv_lon.at[0, slot])
@@ -447,12 +445,8 @@
         for k in range(4):
             load(k, b).start()
 
-    def shift_first(i, carry):
-        for j in range(4):
-            shift_row(4 * i + j, j % 2)
-        return carry
-
-    lax.fori_loop(0, BX // 4, shift_first, 0)
+    for row in range(AHEAD):
+        shift_row(row, row % 2)
 
     def top_rows(b, i, shift):
         x = b * BX + i
@@ -460,8 +454,8 @@
         cell = jnp.concatenate([cells[pl.ds(i + j, HID, stride=PITCH), :] for j in range(2)], axis=1)
         hidden, cell = update(windows(s_top, x, x + 1, 9 * CT, wte), cell)
         for j in range(2):
-            if shift:
-                shift_row(x + BX + j, j)
+            if shift or i + AHEAD < BX:
+                shift_row(x + AHEAD + j, j)
             part = slice(j * TILE, (j + 1) * TILE)
             cells[pl.ds(i + j, HID, stride=PITCH), :] = cell[:, part]
             rows[i + j] = hidden[:, part].astype(BF16)
@@ -492,10 +486,11 @@
                 load(k, b + 5).start()
 
         arrived((2, 3), b)
-        arrived((0, 1, 2, 3), b + 1)
-        arrived((0, 1), b + 2)
+        arrived((0, 1), b + 1)
         before = jnp.maximum(b - 1, 0)
         top_block(b, True, before)
+        arrived((2, 3), b + 1)
+        arrived((0, 1), b + 2)
         top_block(b + 1, True, b)
 
         @pl.when(step > 0)

time: 44.7 us -> 44.4 us (level)
  Pallas kernels: 43.7 us -> 43.2 us
where the time goes in v2:
time: 44.4 us; the launch traced here: 44 us
  Pallas kernels  43.2 us (97%)
  between operations  0.8 us (2%)
    pallas_call x1, Pallas kernels, lower_layer(): pl.pallas_call(lower_kernel, out_shape=(jax.ShapeDtypeStruct((TILE, HID,...  24.4 us
    pallas_call x1, Pallas kernels, upper_layer(): pl.pallas_call(upper_kernel, out_shape=(jax.ShapeDtypeStruct(field, BF16)...  18.8 us

profile of v2, /device:TPU:2, one launch (start us, length us, event | category | flops | bytes accessed | tf_op | source)
XLA Modules:
  0.0 44.0 jit_solution(1605526606417238329)
XLA Ops:
  0.6 24.4 %lower_layer.1 = (bf16[128,64,128]{2,1,0:T(8,128)(2,1)}, bf16[128,64,128]{2,1,0:T(8,128)(2,1)}, f32[8,64,16,128]{3,2,1,0:T(8,128)}, bf16[2,128,128]{2,1,0:T(8,128)(2,1)}, bf16[2,384,128]{2,1,0:T(8,128)(2,1)}) custom-call(bf16[16,128,128]{2,1,0:T(8,128)(2,1)} %bitcast.16, bf16[64,128,128]{2,1,0:T(8,128)(2,1)} %bitcast.14, bf16[64,128,128]{2,1,0:T(8,128)(2,1)} %bitcast.15, ...), custom_call_target="tpu_custom_call" | custom-call | tf_op jit(solution)/shard_map/lower_layer/pallas_call | solution.py:365
  25.1 18.8 %upper_layer.1 = (bf16[64,128,128]{2,1,0:T(8,128)(2,1)}, bf16[64,128,128]{2,1,0:T(8,128)(2,1)}, f32[64,128,128]{2,1,0:T(8,128)}, f32[64,128,128]{2,1,0:T(8,128)}) custom-call(bf16[128,64,128]{2,1,0:T(8,128)(2,1)} %get-tuple-element.13.t_hid, bf16[128,64,128]{2,1,0:T(8,128)(2,1)} %get-tuple-element.14.t_ht, f32[8,64,16,128]{3,2,1,0:T(8,128)} %get-tuple-element.15.co_in, ...), custom_call_target="tpu_custom_call" | custom-call | tf_op jit(solution)/shard_map/upper_layer/pallas_call | solution.py:522

commit v3 on v2

--- a/solution.py
+++ b/solution.py
@@ -87,7 +87,11 @@
     ] + [
         pltpu.make_async_copy(cl.at[:, b * BX:(b + 1) * BX, :], clv.at[b, :, 0:BX, :], sem_in.at[3 + b]) for b in range(NB)
     ]
-    for load in loads[0:2]:
+    pieces = [
+        pltpu.make_async_copy(hl.at[q:q + CIN], hlv.at[q:q + CIN], sem_in.at[3 + NB + q // CIN])
+        for q in range(0, HID, CIN)
+    ]
+    for load in [loads[0]] + pieces:
         load.start()
 
     polars = [lat == 0, lat == nlat - 1]
@@ -139,19 +143,17 @@
             src_ref=src, dst_ref=dst, send_sem=send_sem, recv_sem=recv_sem,
             device_id=lon_targets[0], device_id_type=MESH).wait_recv()
 
-    for load in loads[0:2]:
-        load.wait()
-    for load in loads[2:]:
-        load.start()
+    loads[0].wait()
     for k in range(CIN // 8):
         columns(frv, 0, k)
 
-    def hidden_columns(k, carry):
-        columns(hlv, CIN, 2 * k)
-        columns(hlv, CIN, 2 * k + 1)
-        return carry
-
-    lax.fori_loop(0, HID // 16, hidden_columns, 0)
+    for q in range(HID // CIN):
+        pieces[q].wait()
+        if q == HID // CIN - 1:
+            for load in loads[2:]:
+                load.start()
+        for k in range(CIN // 8):
+            columns(hlv, CIN, q * (CIN // 8) + k)
     for side in range(2):
         near_out[side] = tmp[pl.ds(2 * side, CL, stride=8), :].astype(BF16)
         rest_out[side, 0:CL] = tmp[pl.ds(2 * side + 1, CL, stride=8), :].astype(BF16)
@@ -388,7 +390,7 @@
             pltpu.VMEM((HID * 8, TILE), F32),
             *exchanged,
             *exchanged,
-            pltpu.SemaphoreType.DMA((3 + NB,)),
+            pltpu.SemaphoreType.DMA((3 + NB + HID // CIN,)),
             pltpu.SemaphoreType.DMA((3, NB)),
             pltpu.SemaphoreType.DMA((3, 2)),
             pltpu.SemaphoreType.DMA((3, 2)),

time: 44.4 us -> 44.7 us (level)
  no operation moved by 1% of the time
where the time goes in v3:
time: 44.7 us; the launch traced here: 44.3 us
  Pallas kernels  43.5 us (97%)
  between operations  0.8 us (2%)
    pallas_call x1, Pallas kernels, lower_layer(): pl.pallas_call(lower_kernel, out_shape=(jax.ShapeDtypeStruct((TILE, HID,...  24.7 us
    pallas_call x1, Pallas kernels, upper_layer(): pl.pallas_call(upper_kernel, out_shape=(jax.ShapeDtypeStruct(field, BF16)...  18.7 us

profile of v3, /device:TPU:2, one launch (start us, length us, event | category | flops | bytes accessed | tf_op | source)
XLA Modules:
  0.0 44.3 jit_solution(641120863754132399)
XLA Ops:
  0.6 24.7 %lower_layer.1 = (bf16[128,64,128]{2,1,0:T(8,128)(2,1)}, bf16[128,64,128]{2,1,0:T(8,128)(2,1)}, f32[8,64,16,128]{3,2,1,0:T(8,128)}, bf16[2,128,128]{2,1,0:T(8,128)(2,1)}, bf16[2,384,128]{2,1,0:T(8,128)(2,1)}) custom-call(bf16[16,128,128]{2,1,0:T(8,128)(2,1)} %bitcast.16, bf16[64,128,128]{2,1,0:T(8,128)(2,1)} %bitcast.14, bf16[64,128,128]{2,1,0:T(8,128)(2,1)} %bitcast.15, ...), custom_call_target="tpu_custom_call" | custom-call | tf_op jit(solution)/shard_map/lower_layer/pallas_call | solution.py:367
  25.4 18.7 %upper_layer.1 = (bf16[64,128,128]{2,1,0:T(8,128)(2,1)}, bf16[64,128,128]{2,1,0:T(8,128)(2,1)}, f32[64,128,128]{2,1,0:T(8,128)}, f32[64,128,128]{2,1,0:T(8,128)}) custom-call(bf16[128,64,128]{2,1,0:T(8,128)(2,1)} %get-tuple-element.13.t_hid, bf16[128,64,128]{2,1,0:T(8,128)(2,1)} %get-tuple-element.14.t_ht, f32[8,64,16,128]{3,2,1,0:T(8,128)} %get-tuple-element.15.co_in, ...), custom_call_target="tpu_custom_call" | custom-call | tf_op jit(solution)/shard_map/upper_layer/pallas_call | solution.py:524
